TPU v7x, 32 devices: a whole 2x2x4 slice. The times are simulated.
32 devices in a mesh: rep: 4 (over z), exp: 8 (over y, x, core).
Axes of the slice: x: 2, y: 2, z: 4, core: 2. Of those that a mesh axis runs over, the one named last changes fastest.
Arguments:
- tokens: bfloat16 [36864, 768], P(('rep', 'exp')), may hold values from -6 to 6
- cotangent: bfloat16 [36864, 768], P(('rep', 'exp')), may hold values from -6 to 6
- expert_ids: int32 [36864, 2], P(('rep', 'exp')), may hold values from 0 to 7, as said below
- expert_slots: int32 [36864, 2], P(('rep', 'exp')), may hold values from -1 to 143, as said below
- w_qkv: bfloat16 [768, 2304], replicated, may hold values from -0.21875 to 0.21875
- q_bias: bfloat16 [768], replicated, may hold values from -1.75 to 1.75
- v_bias: bfloat16 [768], replicated, may hold values from -1.75 to 1.75
- w_proj: bfloat16 [768, 768], replicated, may hold values from -0.875 to 0.875
- proj_bias: bfloat16 [768], replicated, may hold values from -1.75 to 1.75
- gain_one: float32 [768], replicated, may hold values from 0.25 to 1.75
- shift_one: float32 [768], replicated, may hold values from -1.75 to 1.75
- gain_two: float32 [768], replicated, may hold values from 0.25 to 1.75
- shift_two: float32 [768], replicated, may hold values from -1.75 to 1.75
- w_router: float32 [768, 8], replicated, may hold values from -0.15625 to 0.15625
- expert_in: bfloat16 [8, 768, 3072], P('exp'), may hold values from -0.21875 to 0.21875
- expert_in_bias: bfloat16 [8, 3072], P('exp'), may hold values from -1.75 to 1.75
- expert_out: bfloat16 [8, 3072, 768], P('exp'), may hold values from -0.4375 to 0.4375
- expert_out_bias: bfloat16 [8, 768], P('exp'), may hold values from -1.5 to 1.5
Outputs:
- mixed: bfloat16 [36864, 768], P(('rep', 'exp'))
- grad_tokens: float32 [36864, 768], P(('rep', 'exp'))
- grad_w_qkv: float32 [768, 2304], replicated
- grad_q_bias: float32 [768], replicated
- grad_v_bias: float32 [768], replicated
- grad_w_proj: float32 [768, 768], replicated
- grad_proj_bias: float32 [768], replicated
- grad_gain_one: float32 [768], replicated
- grad_shift_one: float32 [768], replicated
- grad_gain_two: float32 [768], replicated
- grad_shift_two: float32 [768], replicated
- grad_w_router: float32 [768, 8], replicated
- grad_expert_in: float32 [8, 768, 3072], P('exp', None, 'rep')
- grad_expert_in_bias: float32 [8, 3072], P('exp', 'rep')
- grad_expert_out: float32 [8, 3072, 768], P('exp', 'rep')
- grad_expert_out_bias: float32 [8, 768], P('exp', 'rep')
Inputs may be any that keep to these rules, and one draw needn't show every extreme that they name: `expert_ids`: the two experts of a patch differ. `expert_slots`: among the pairs of one device (aligned blocks of 1152 rows), each expert's kept pairs hold the slots 0, 1, 2, ... once each in a priority order of those pairs, and a pair is -1 exactly when its expert already has 144 pairs of that device before it.
All inputs are finite; a program needn't handle non-finite values.
Results may differ from a plain program's by a relative error of at most 0.014.
Values may be sent and summed in bfloat16 or wider, within the bound.
No kernel may reach another device: no remote copies, remote signals or barrier semaphores. Data moves between devices by JAX's collectives and lax.ppermute only.
A program may use at most 192 MiB of HBM per device.

v0:
```python
import jax
import jax.numpy as jnp
from jax import lax
from jax.sharding import PartitionSpec as P

HEADS = 12
HEAD_DIM = 64
SEQ = 576
EPSILON = 1e-06
HIGHEST = lax.Precision.HIGHEST


def norm_forward(field, norm_gain, norm_shift):
    average = jnp.mean(field, axis=-1, keepdims=True)
    centred = field - average
    variance = jnp.mean(centred * centred, axis=-1, keepdims=True)
    inverse = lax.rsqrt(variance + EPSILON)
    unit_rows = centred * inverse
    return (unit_rows * norm_gain + norm_shift, unit_rows, inverse)


def norm_backward(grad_out, unit_rows, inverse, norm_gain):
    grad_unit = grad_out * norm_gain
    centred = grad_unit - jnp.mean(grad_unit, axis=-1, keepdims=True)
    along = unit_rows * jnp.mean(grad_unit * unit_rows, axis=-1, keepdims=True)
    return (
        inverse * (centred - along),
        jnp.sum(grad_out * unit_rows, axis=0),
        jnp.sum(grad_out, axis=0),
    )


def by_heads(block):
    return block.reshape(block.shape[0], HEADS, HEAD_DIM)


def contract_last(left, right):
    return lax.dot_general(
        left, right, (((1,), (1,)), ((), ())), preferred_element_type=jnp.float32
    )


def contract_first(left, right):
    return lax.dot_general(
        left, right, (((0,), (0,)), ((), ())), preferred_element_type=jnp.float32
    )


def contract_first_high(left, right):
    return lax.dot_general(
        left, right, (((0,), (0,)), ((), ())), precision=HIGHEST, preferred_element_type=jnp.float32
    )


def exact_gelu(field):
    return jax.nn.gelu(field, approximate=False)


def image_scores(queries, key_rows):
    return jnp.einsum(
        "qhd,khd->hqk", by_heads(queries), by_heads(key_rows), preferred_element_type=jnp.float32
    ) * HEAD_DIM ** (-0.5)


def attend_image(pieces):
    queries, key_rows, values = pieces
    scores = image_scores(queries, key_rows)
    row_max = jnp.max(scores, axis=-1, keepdims=True)
    exponent = jnp.exp(scores - row_max)
    row_total = jnp.sum(exponent, axis=-1, keepdims=True)
    weights = (exponent / row_total).astype(jnp.bfloat16)
    context = jnp.einsum(
        "hqk,khd->qhd", weights, by_heads(values), preferred_element_type=jnp.float32
    )
    return (context.reshape(queries.shape[0], -1), (row_max + jnp.log(row_total))[..., 0])


def attend_back(pieces):
    queries, key_rows, values, grad_context, log_total = pieces
    scores = image_scores(queries, key_rows)
    probs = jnp.exp(scores - log_total[..., None])
    weights = probs.astype(jnp.bfloat16)
    grad_heads = by_heads(grad_context)
    grad_probs = jnp.einsum(
        "qhd,khd->hqk", grad_heads, by_heads(values), preferred_element_type=jnp.float32
    )
    grad_values = jnp.einsum(
        "hqk,qhd->khd", weights, grad_heads, preferred_element_type=jnp.float32
    )
    grad_scores = (
        probs * (grad_probs - jnp.sum(probs * grad_probs, axis=-1, keepdims=True))
    ).astype(jnp.bfloat16)
    grad_queries = jnp.einsum(
        "hqk,khd->qhd", grad_scores, by_heads(key_rows), preferred_element_type=jnp.float32
    ) * HEAD_DIM ** (-0.5)
    grad_keys = jnp.einsum(
        "hqk,qhd->khd", grad_scores, by_heads(queries), preferred_element_type=jnp.float32
    ) * HEAD_DIM ** (-0.5)
    length = queries.shape[0]
    joined = jnp.concatenate(
        [
            grad_queries.reshape(length, -1),
            grad_keys.reshape(length, -1),
            grad_values.reshape(length, -1),
        ],
        axis=1,
    )
    return joined.astype(jnp.bfloat16)


def expert_backward(rows_in, grads_out, weight_in, bias_in, weight_out):
    hidden = jnp.dot(rows_in, weight_in, preferred_element_type=jnp.float32) + bias_in
    activated, gelu_back = jax.vjp(exact_gelu, hidden)
    grad_hidden = gelu_back(contract_last(grads_out, weight_out))[0].astype(jnp.bfloat16)
    return (activated.astype(jnp.bfloat16), grad_hidden)


def on_device(
    tokens,
    cotangent,
    expert_ids,
    expert_slots,
    w_qkv,
    q_bias,
    v_bias,
    w_proj,
    proj_bias,
    gain_one,
    shift_one,
    gain_two,
    shift_two,
    w_router,
    expert_in,
    expert_in_bias,
    expert_out,
    expert_out_bias,
):
    row_count, model_width = tokens.shape
    experts = w_router.shape[1]
    slot_count = row_count // experts
    images = row_count // SEQ
    inputs = tokens.astype(jnp.float32)
    normed_one, unit_one, inverse_one = norm_forward(inputs, gain_one, shift_one)
    normed_one = normed_one.astype(jnp.bfloat16)
    bias_row = jnp.concatenate(
        [
            q_bias.astype(jnp.float32),
            jnp.zeros((model_width,), jnp.float32),
            v_bias.astype(jnp.float32),
        ]
    )
    projected = (jnp.dot(normed_one, w_qkv, preferred_element_type=jnp.float32) + bias_row).astype(
        jnp.bfloat16
    )
    image_blocks = projected.reshape(images, SEQ, 3 * model_width)
    query_blocks = image_blocks[:, :, :model_width]
    key_blocks = image_blocks[:, :, model_width : 2 * model_width]
    value_blocks = image_blocks[:, :, 2 * model_width :]
    context, log_total = lax.map(attend_image, (query_blocks, key_blocks, value_blocks))
    context = context.reshape(row_count, model_width).astype(jnp.bfloat16)
    branch = jnp.dot(context, w_proj, preferred_element_type=jnp.float32) + proj_bias.astype(
        jnp.float32
    )
    residual = inputs + branch
    normed_two, unit_two, inverse_two = norm_forward(residual, gain_two, shift_two)
    normed_two = normed_two.astype(jnp.bfloat16)
    router = jax.nn.softmax(
        jnp.dot(normed_two.astype(jnp.float32), w_router, precision=HIGHEST), axis=-1
    )
    columns = jnp.where(expert_slots >= 0, expert_ids * slot_count + expert_slots, -1)
    target = lax.broadcasted_iota(jnp.int32, (1, experts * slot_count), 1)
    first_hit = (columns[:, 0:1] == target).astype(jnp.bfloat16)
    second_hit = (columns[:, 1:2] == target).astype(jnp.bfloat16)
    either = first_hit + second_hit
    hits = jnp.concatenate([first_hit, second_hit], axis=0)
    chosen = (expert_ids[:, :, None] == lax.broadcasted_iota(jnp.int32, (1, 1, experts), 2)).astype(
        jnp.float32
    )
    gate_values = jnp.sum(router[:, None, :] * chosen, axis=-1)
    outgoing = (
        contract_first(either, normed_two)
        .astype(jnp.bfloat16)
        .reshape(experts, slot_count, model_width)
    )
    arrived = lax.all_to_all(outgoing, "exp", split_axis=0, concat_axis=0, tiled=True).reshape(
        row_count, model_width
    )
    weight_in = expert_in[0]
    bias_in = expert_in_bias[0].astype(jnp.float32)
    weight_out = expert_out[0]
    bias_out = expert_out_bias[0].astype(jnp.float32)
    hidden = jnp.dot(arrived, weight_in, preferred_element_type=jnp.float32) + bias_in
    activated = exact_gelu(hidden).astype(jnp.bfloat16)
    produced = (
        jnp.dot(activated, weight_out, preferred_element_type=jnp.float32) + bias_out
    ).astype(jnp.bfloat16)
    returned = lax.all_to_all(
        produced.reshape(experts, slot_count, model_width),
        "exp",
        split_axis=0,
        concat_axis=0,
        tiled=True,
    ).reshape(row_count, model_width)
    picked_both = jnp.dot(hits, returned, preferred_element_type=jnp.float32)
    picked_first = picked_both[:row_count]
    picked_second = picked_both[row_count:]
    final = residual + gate_values[:, 0:1] * picked_first + gate_values[:, 1:2] * picked_second
    mixed = final.astype(jnp.bfloat16)
    grad_out = cotangent.astype(jnp.float32)
    grad_gates = jnp.stack(
        [jnp.sum(grad_out * picked_first, axis=-1), jnp.sum(grad_out * picked_second, axis=-1)],
        axis=-1,
    )
    grad_router = jnp.sum(grad_gates[:, :, None] * chosen, axis=1)
    grad_logits = router * (grad_router - jnp.sum(router * grad_router, axis=-1, keepdims=True))
    grad_picked = jnp.concatenate(
        [gate_values[:, 0:1] * grad_out, gate_values[:, 1:2] * grad_out], axis=0
    ).astype(jnp.bfloat16)
    grad_returned = (
        contract_first(hits, grad_picked)
        .astype(jnp.bfloat16)
        .reshape(experts, slot_count, model_width)
    )
    grad_produced = lax.all_to_all(
        grad_returned, "exp", split_axis=0, concat_axis=0, tiled=True
    ).reshape(row_count, model_width)
    act_round, grad_hidden = expert_backward(arrived, grad_produced, weight_in, bias_in, weight_out)
    grad_arrived = (
        contract_last(grad_hidden, weight_in)
        .astype(jnp.bfloat16)
        .reshape(experts, slot_count, model_width)
    )
    grad_source = lax.all_to_all(
        grad_arrived, "exp", split_axis=0, concat_axis=0, tiled=True
    ).reshape(row_count, model_width)
    local_in = contract_first(arrived, grad_hidden)[None]
    local_in_bias = jnp.sum(grad_hidden.astype(jnp.float32), axis=0)[None]
    local_out = contract_first(act_round, grad_produced)[None]
    local_out_bias = jnp.sum(grad_produced.astype(jnp.float32), axis=0)[None]
    grad_ein, grad_einb, grad_eout, grad_eoutb = (
        lax.psum_scatter(
            local_in.astype(jnp.bfloat16), "rep", scatter_dimension=2, tiled=True
        ).astype(jnp.float32),
        lax.psum_scatter(
            local_in_bias.astype(jnp.bfloat16), "rep", scatter_dimension=1, tiled=True
        ).astype(jnp.float32),
        lax.psum_scatter(
            local_out.astype(jnp.bfloat16), "rep", scatter_dimension=1, tiled=True
        ).astype(jnp.float32),
        lax.psum_scatter(
            local_out_bias.astype(jnp.bfloat16), "rep", scatter_dimension=1, tiled=True
        ).astype(jnp.float32),
    )
    grad_normed_two = jnp.dot(either, grad_source, preferred_element_type=jnp.float32)
    grad_normed_two = grad_normed_two + lax.dot_general(
        grad_logits,
        w_router,
        (((1,), (1,)), ((), ())),
        precision=HIGHEST,
        preferred_element_type=jnp.float32,
    )
    local_router = contract_first_high(normed_two.astype(jnp.float32), grad_logits)
    grad_from_norm, local_gain_two, local_shift_two = norm_backward(
        grad_normed_two, unit_two, inverse_two, gain_two
    )
    grad_residual = grad_out + grad_from_norm
    grad_branch = grad_residual.astype(jnp.bfloat16)
    local_proj = contract_first(context, grad_branch)
    local_proj_bias = jnp.sum(grad_branch.astype(jnp.float32), axis=0)
    grad_context = contract_last(grad_branch, w_proj).astype(jnp.bfloat16)
    grad_qkv = lax.map(
        attend_back,
        (
            query_blocks,
            key_blocks,
            value_blocks,
            grad_context.reshape(images, SEQ, model_width),
            log_total,
        ),
    )
    grad_qkv = grad_qkv.reshape(row_count, 3 * model_width)
    local_qkv = contract_first(normed_one, grad_qkv)
    grad_wide = grad_qkv.astype(jnp.float32)
    local_q_bias = jnp.sum(grad_wide[:, :model_width], axis=0)
    local_v_bias = jnp.sum(grad_wide[:, 2 * model_width :], axis=0)
    grad_normed_one = contract_last(grad_qkv, w_qkv)
    grad_from_first, local_gain_one, local_shift_one = norm_backward(
        grad_normed_one, unit_one, inverse_one, gain_one
    )
    grad_tokens = grad_residual + grad_from_first
    (
        grad_w_qkv,
        grad_q_bias,
        grad_v_bias,
        grad_w_proj,
        grad_proj_bias,
        grad_gain_one,
        grad_shift_one,
        grad_gain_two,
        grad_shift_two,
        grad_w_router,
    ) = lax.psum(
        (
            local_qkv,
            local_q_bias,
            local_v_bias,
            local_proj,
            local_proj_bias,
            local_gain_one,
            local_shift_one,
            local_gain_two,
            local_shift_two,
            local_router,
        ),
        ("rep", "exp"),
    )
    return (
        mixed,
        grad_tokens,
        grad_w_qkv,
        grad_q_bias,
        grad_v_bias,
        grad_w_proj,
        grad_proj_bias,
        grad_gain_one,
        grad_shift_one,
        grad_gain_two,
        grad_shift_two,
        grad_w_router,
        grad_ein,
        grad_einb,
        grad_eout,
        grad_eoutb,
    )


def solution(mesh):
    placed = (
        P(("rep", "exp"), None),
        P(("rep", "exp"), None),
        P(("rep", "exp"), None),
        P(("rep", "exp"), None),
        P(),
        P(),
        P(),
        P(),
        P(),
        P(),
        P(),
        P(),
        P(),
        P(),
        P("exp", None, None),
        P("exp", None),
        P("exp", None, None),
        P("exp", None),
    )
    return jax.shard_map(
        on_device,
        mesh=mesh,
        in_specs=placed,
        out_specs=(
            P(("rep", "exp"), None),
            P(("rep", "exp"), None),
            P(),
            P(),
            P(),
            P(),
            P(),
            P(),
            P(),
            P(),
            P(),
            P(),
            P("exp", None, "rep"),
            P("exp", "rep"),
            P("exp", "rep", None),
            P("exp", "rep"),
        ),
        check_vma=False,
    )
```

profile of v0, /device:TPU:0, one launch (start us, length us, event | category | flops | bytes accessed | tf_op | source)
XLA Modules:
  0.0 720.9 jit_solution(12045565676149617166)
XLA Ops:
  40.2 76.1 %while.22 = (s32[]{:T(128)}, bf16[2,576,768]{2,1,0:T(8,128)(2,1)}, f32[2,12,576]{2,1,0:T(8,128)}, bf16[2,576,768]{1,2,0:T(8,128)(2,1)}, bf16[2,576,768]{1,2,0:T(...) while((s32[]{:T(128)}, bf16[2,576,768]{2,1,0:T(8,128)(2,1)}, f32[2,12,576]{2,1,0:T(8,128)}, ...), condition=%wide.region_5.6_spmd, body=%wide.region_2.5_spmd.sunk | while | flops 1055040768 | bytes 61086932 | solution.py:159
  52.4 9.7 %fusion.143 = f32[12,576]{1,0:T(8,128)} fusion(f32[12,576,576]{1,2,0:T(8,128)} %get-tuple-element.347, f32[12,576]{1,0:T(8,128)} %get-tuple-element.348), kind=kLoop, calls=%fused_computation.3.clone.1 | loop fusion | flops 11937024 | bytes 15980544 | tf_op jit(solution)/shard_map/while/body/eval_jaxpr/reduce_sum | solution.py:70
  62.1 11.1 %fusion.144 = bf16[12,64,576]{2,1,0:T(8,128)(2,1)} fusion(bf16[576,12,64]{0,2,1:T(8,128)(2,1)} %bitcast.167, f32[12,576,576]{1,2,0:T(8,128)} %get-tuple-element.347, f32[12,576]{1,0:T(8,128)} %fusion.143, f32[12,576]{1,0:T(8,128)} %get-tuple-element.348), kind=kOutput, calls=%fused_computation.4.clone.1 | convolution fusion | flops 525533184 | bytes 17750016 | tf_op jit(solution)/shard_map/while/body/eval_jaxpr/hqk,khd->qhd/dot_general | solution.py:72
  90.1 9.7 %fusion.143 = f32[12,576]{1,0:T(8,128)} fusion(f32[12,576,576]{1,2,0:T(8,128)} %get-tuple-element.347, f32[12,576]{1,0:T(8,128)} %get-tuple-element.348), kind=kLoop, calls=%fused_computation.3.clone.1 | loop fusion | flops 11937024 | bytes 15980544 | tf_op jit(solution)/shard_map/while/body/eval_jaxpr/reduce_sum | solution.py:70
  99.8 11.1 %fusion.144 = bf16[12,64,576]{2,1,0:T(8,128)(2,1)} fusion(bf16[576,12,64]{0,2,1:T(8,128)(2,1)} %bitcast.167, f32[12,576,576]{1,2,0:T(8,128)} %get-tuple-element.347, f32[12,576]{1,0:T(8,128)} %fusion.143, f32[12,576]{1,0:T(8,128)} %get-tuple-element.348), kind=kOutput, calls=%fused_computation.4.clone.1 | convolution fusion | flops 525533184 | bytes 17750016 | tf_op jit(solution)/shard_map/while/body/eval_jaxpr/hqk,khd->qhd/dot_general | solution.py:72
  141.2 14.5 %all-to-all-done = bf16[8,144,768]{2,1,0:T(8,128)(2,1)} async-done(((bf16[8,144,768]{2,1,0:T(8,128)(2,1)}), bf16[8,144,768]{2,1,0:T(8,128)(2,1)}, u32[]{:S(2)}, u32[]{:S(2)}) %all-to-all-start) | async-done | bytes 1769504 | tf_op jit(solution)/shard_map/all_to_all | solution.py:185
  155.7 40.7 %multiply_convert_fusion.3 = (bf16[1152,3072]{1,0:T(8,128)(2,1)S(1)}, f32[1152,3072]{1,0:T(8,128)}, f32[1152,3072]{1,0:T(8,128)}) fusion(f32[3072]{0:T(1024)S(1)} %bitcast.180, bf16[1152,768]{1,0:T(8,128)(2,1)} %bitcast.20, bf16[1,768,3072]{2,1,0:T(8,128)(2,1)} %param.36), kind=kOutput, calls=%fused_computation.32 | convolution fusion | flops 5669388288 | bytes 41889792 | tf_op jit(solution)/shard_map/dot_general | solution.py:192
  213.1 17.7 %all-to-all-done.1 = bf16[8,144,768]{2,1,0:T(8,128)(2,1)} async-done(((bf16[8,144,768]{2,1,0:T(8,128)(2,1)}), bf16[8,144,768]{2,1,0:T(8,128)(2,1)}, u32[]{:S(2)}, u32[]{:S(2)}) %all-to-all-start.1) | async-done | bytes 1769504 | tf_op jit(solution)/shard_map/all_to_all | solution.py:197
  248.6 26.2 %all_to_all.20 = bf16[8,144,768]{2,1,0:T(8,128)(2,1)} all-to-all(bf16[8,144,768]{2,1,0:T(8,128)(2,1)S(1)} %bitcast.177), channel_id=1, replica_groups=mesh['rep'=4,'exp'=8] {'exp'}, dimensions={0} | all-to-all | bytes 3538944 | tf_op jit(solution)/shard_map/all_to_all | solution.py:224
  278.8 20.9 %fusion.86 = (bf16[3072]{0:T(1024)(128)(2,1)}, bf16[1152,3072]{1,0:T(8,128)(2,1)}) fusion(f32[1152,3072]{1,0:T(8,128)} %get-tuple-element.237, f32[1152,3072]{1,0:T(8,128)} %get-tuple-element.254, bf16[1152,768]{1,0:T(8,128)(2,1)} %bitcast.169, bf16[1,3072,768]{2,1,0:T(8,128)(2,1)} %param.38), kind=kOutput, calls=%fused_computation.154 | convolution fusion | flops 5488899072 | bytes 41883648 | tf_op jit(solution)/shard_map/dot_general | solution.py:38
  301.8 10.6 %fusion.28 = bf16[1,3072,768]{2,1,0:T(8,128)(2,1)} fusion(bf16[1152,3072]{1,0:T(8,128)(2,1)} %copy-done.59, bf16[1152,768]{1,0:T(8,128)(2,1)} %bitcast.170), kind=kOutput, calls=%fused_computation.71 | convolution fusion | flops 5438177280 | bytes 13565952 | tf_op jit(solution)/shard_map/dot_general | solution.py:44
  313.9 10.3 %fusion.55 = bf16[1152,768]{1,0:T(8,128)(2,1)} fusion(bf16[1152,3072]{1,0:T(8,128)(2,1)} %get-tuple-element.261, bf16[1,768,3072]{2,1,0:T(8,128)(2,1)} %param.36), kind=kOutput, calls=%fused_computation.106 | convolution fusion | flops 5436702720 | bytes 13565952 | tf_op jit(solution)/shard_map/dot_general | solution.py:38
  332.3 11.2 %fusion.27 = bf16[1,768,3072]{2,1,0:T(8,128)(2,1)} fusion(bf16[1152,768]{1,0:T(8,128)(2,1)} %bitcast.20, bf16[1152,3072]{1,0:T(8,128)(2,1)} %get-tuple-element.261), kind=kOutput, calls=%fused_computation.70 | convolution fusion | flops 5438177280 | bytes 13565952 | tf_op jit(solution)/shard_map/dot_general | solution.py:44
  372.1 131.4 %while.23 = (s32[]{:T(128)}, bf16[2,576,2304]{2,1,0:T(8,128)(2,1)}, bf16[2,576,768]{1,2,0:T(8,128)(2,1)}, bf16[2,576,768]{1,2,0:T(8,128)(2,1)}, f32[2,12,576]{2,...) while((s32[]{:T(128)}, bf16[2,576,2304]{2,1,0:T(8,128)(2,1)}, ...), condition=%wide.region_19.20_spmd, body=%wide.region_17.19_spmd.sunk | while | flops 2605982976 | bytes 160441552 | solution.py:271
  388.7 10.2 %fusion.156 = bf16[12,64,576]{2,1,0:T(8,128)(2,1)} fusion(bf16[576,12,64]{0,2,1:T(8,128)(2,1)S(1)} %bitcast.154, f32[12,576,576]{1,2,0:T(8,128)} %fusion.155, f32[12,576]{1,0:T(8,128)S(1)} %copy-done.11), kind=kOutput, calls=%fused_computation.21.clone.1 | convolution fusion | flops 521994240 | bytes 17722368 | tf_op jit(solution)/shard_map/while/body/eval_jaxpr/hqk,qhd->khd/dot_general | solution.py:87
  398.9 11.7 %multiply_reduce_fusion.11 = (f32[12,576]{1,0:T(8,128)S(1)}, f32[12,576,576]{1,2,0:T(8,128)}) fusion(f32[12,576,576]{1,2,0:T(8,128)} %fusion.155, f32[12,576]{1,0:T(8,128)S(1)} %copy-done.11, bf16[576,12,64]{0,2,1:T(8,128)(2,1)S(1)} %bitcast.155, bf16[576,12,64]{0,2,1:T(8,128)(2,1)S(1)} %bitcast.160), kind=kOutput, calls=%fused_computation.12.clone.1 | convolution fusion | flops 525526272 | bytes 33675264 | tf_op jit(solution)/shard_map/while/body/eval_jaxpr/qhd,khd->hqk/dot_general | solution.py:84
  410.6 13.3 %multiply_convert_fusion.7 = bf16[12,576,576]{1,2,0:T(8,128)(2,1)S(1)} fusion(f32[12,576,576]{1,2,0:T(8,128)} %get-tuple-element.358, f32[12,576,576]{1,2,0:T(8,128)} %fusion.155, f32[12,576]{1,0:T(8,128)S(1)} %get-tuple-element.359, f32[12,576]{1,0:T(8,128)S(1)} %copy-done.11), kind=kLoop, calls=%fused_computation.11.clone.1 | loop fusion | flops 19906560 | bytes 39868416 | tf_op jit(solution)/shard_map/while/body/eval_jaxpr/convert_element_type | solution.py:92
  454.6 10.2 %fusion.156 = bf16[12,64,576]{2,1,0:T(8,128)(2,1)} fusion(bf16[576,12,64]{0,2,1:T(8,128)(2,1)S(1)} %bitcast.154, f32[12,576,576]{1,2,0:T(8,128)} %fusion.155, f32[12,576]{1,0:T(8,128)S(1)} %copy-done.11), kind=kOutput, calls=%fused_computation.21.clone.1 | convolution fusion | flops 521994240 | bytes 17722368 | tf_op jit(solution)/shard_map/while/body/eval_jaxpr/hqk,qhd->khd/dot_general | solution.py:87
  464.8 11.7 %multiply_reduce_fusion.11 = (f32[12,576]{1,0:T(8,128)S(1)}, f32[12,576,576]{1,2,0:T(8,128)}) fusion(f32[12,576,576]{1,2,0:T(8,128)} %fusion.155, f32[12,576]{1,0:T(8,128)S(1)} %copy-done.11, bf16[576,12,64]{0,2,1:T(8,128)(2,1)S(1)} %bitcast.155, bf16[576,12,64]{0,2,1:T(8,128)(2,1)S(1)} %bitcast.160), kind=kOutput, calls=%fused_computation.12.clone.1 | convolution fusion | flops 525526272 | bytes 33675264 | tf_op jit(solution)/shard_map/while/body/eval_jaxpr/qhd,khd->hqk/dot_general | solution.py:84
  476.6 12.5 %multiply_convert_fusion.7 = bf16[12,576,576]{1,2,0:T(8,128)(2,1)S(1)} fusion(f32[12,576,576]{1,2,0:T(8,128)} %get-tuple-element.358, f32[12,576,576]{1,2,0:T(8,128)} %fusion.155, f32[12,576]{1,0:T(8,128)S(1)} %get-tuple-element.359, f32[12,576]{1,0:T(8,128)S(1)} %copy-done.11), kind=kLoop, calls=%fused_computation.11.clone.1 | loop fusion | flops 19906560 | bytes 39868416 | tf_op jit(solution)/shard_map/while/body/eval_jaxpr/convert_element_type | solution.py:92
  503.5 11.1 %fusion.78 = f32[768,2304]{1,0:T(8,128)} fusion(bf16[1152,2304]{1,0:T(8,128)(2,1)} %bitcast.172, bf16[1152,768]{0,1:T(8,128)(2,1)} %copy.98, f32[768]{0:T(1024)} %param.32, f32[768]{0:T(1024)} %param.31, f32[1152]{0:T(1024)S(1)} %copy-done.39, f32[1152]{0:T(1024)S(1)} %copy-done.32), kind=kOutput, calls=%fused_computation.149 | convolution fusion | flops 4082171904 | bytes 14171136 | tf_op jit(solution)/shard_map/dot_general | solution.py:44
  514.6 9.2 %fusion.85 = (f32[768]{0:T(1024)}, f32[1152,768]{1,0:T(8,128)}) fusion(bf16[1152,2304]{1,0:T(8,128)(2,1)} %bitcast.173, bf16[768,2304]{1,0:T(8,128)(2,1)S(1)} %copy-done), kind=kOutput, calls=%fused_computation.153 | convolution fusion | flops 4077747456 | bytes 12389376 | tf_op jit(solution)/shard_map/dot_general | solution.py:38
  551.8 41.6 %all-reduce = (f32[768]{0:T(1024)}, f32[768]{0:T(1024)}, f32[768]{0:T(1024)}, f32[768]{0:T(1024)}, f32[768]{0:T(1024)}, /*index=5*/f32[768]{0:T(1024)}, f32[768]{0:T(1024)}, f32[768,8]{0,1:T(8,128)}) all-reduce(f32[768]{0:T(1024)S(1)} %get-tuple-element.182, ...), channel_id=1, replica_groups=mesh['rep'=4,'exp'=8] {'rep','exp'}, use_global_device_ids=true, to_apply=%region_24.25 | all-reduce | flops 11520 | bytes 92160 | tf_op jit(solution)/shard_map/psum | solution.py:302
  599.2 106.4 %all-reduce.4.cloned.1.call-done = (f32[768,2304]{1,0:T(8,128)}, f32[768,768]{1,0:T(8,128)}) async-done(((f32[768,2304]{1,0:T(8,128)}, f32[768,768]{1,0:T(8,128)}), (f32[768,2304]{1,0:T(8,128)}, f32[768,768]{1,0:T(8,128)})) %all-reduce.4.cloned.1.call-update) | async-done | bytes 9437200 | tf_op jit(solution)/shard_map/psum | solution.py:302
  (263 shorter events, 271.6 us)
Async XLA Ops:
  8.0 12.2 %copy-start = (bf16[768,2304]{1,0:T(8,128)(2,1)S(1)}, bf16[768,2304]{1,0:T(8,128)(2,1)}, u32[]{:S(2)}) copy-start(bf16[768,2304]{1,0:T(8,128)(2,1)} %param.26) | copy-start | bytes 10616836
  40.2 76.2 %copy-start.52 = (f32[768]{0:T(1024)S(1)}, f32[768]{0:T(1024)}, u32[]{:S(2)}) copy-start(f32[768]{0:T(1024)} %convert_element_type.153) | copy-start | bytes 9220
  62.1 11.1 %copy-start.14 = (f32[12,576]{1,0:T(8,128)S(1)}, f32[12,576]{1,0:T(8,128)}, u32[]{:S(2)}) copy-start(f32[12,576]{1,0:T(8,128)} %get-tuple-element.348) | copy-start | bytes 82948 | tf_op jit(solution)/shard_map/while
  62.1 11.1 %copy-start.15 = (f32[12,576]{1,0:T(8,128)S(1)}, f32[12,576]{1,0:T(8,128)}, u32[]{:S(2)}) copy-start(f32[12,576]{1,0:T(8,128)} %fusion.143) | copy-start | bytes 82948 | tf_op jit(solution)/shard_map/while
  62.1 11.1 %copy-start.23 = (f32[2,12,576]{2,1,0:T(8,128)S(1)}, f32[2,12,576]{2,1,0:T(8,128)}, u32[]{:S(2)}) copy-start(f32[2,12,576]{2,1,0:T(8,128)} %get-tuple-element.369) | copy-start | bytes 165892 | tf_op jit(solution)/shard_map/while
  99.8 11.1 %copy-start.14 = (f32[12,576]{1,0:T(8,128)S(1)}, f32[12,576]{1,0:T(8,128)}, u32[]{:S(2)}) copy-start(f32[12,576]{1,0:T(8,128)} %get-tuple-element.348) | copy-start | bytes 82948 | tf_op jit(solution)/shard_map/while
  99.8 11.1 %copy-start.15 = (f32[12,576]{1,0:T(8,128)S(1)}, f32[12,576]{1,0:T(8,128)}, u32[]{:S(2)}) copy-start(f32[12,576]{1,0:T(8,128)} %fusion.143) | copy-start | bytes 82948 | tf_op jit(solution)/shard_map/while
  99.8 11.1 %copy-start.23 = (f32[2,12,576]{2,1,0:T(8,128)S(1)}, f32[2,12,576]{2,1,0:T(8,128)}, u32[]{:S(2)}) copy-start(f32[2,12,576]{2,1,0:T(8,128)} %get-tuple-element.369) | copy-start | bytes 165892 | tf_op jit(solution)/shard_map/while
  126.9 10.1 %copy-start.54 = (bf16[1,768]{1,0:T(2,128)(2,1)S(1)}, bf16[1,768]{1,0:T(2,128)(2,1)}, u32[]{:S(2)}) copy-start(bf16[1,768]{1,0:T(2,128)(2,1)} %param.39) | copy-start | bytes 4612
  127.0 28.7 %all-to-all-start = ((bf16[8,144,768]{2,1,0:T(8,128)(2,1)}), bf16[8,144,768]{2,1,0:T(8,128)(2,1)}, u32[]{:S(2)}, u32[]{:S(2)}) async-start(bf16[8,144,768]{2,1,0:T(8,128)(2,1)} %bitcast.175), calls=%async_computation | async-start | bytes 3538944 | tf_op jit(solution)/shard_map/all_to_all | solution.py:185
  133.1 22.6 %copy-start.50 = (f32[1,3072]{1,0:T(1,128)S(1)}, f32[1,3072]{1,0:T(1,128)}, u32[]{:S(2)}) copy-start(f32[1,3072]{1,0:T(1,128)} %add.177) | copy-start | bytes 36868
  155.7 40.7 %copy-start.51 = (f32[768]{0:T(1024)S(1)}, f32[768]{0:T(1024)}, u32[]{:S(2)}) copy-start(f32[768]{0:T(1024)} %convert_reduce_fusion.2) | copy-start | bytes 9220
  155.7 40.7 %copy-start.55 = (bf16[1,3072,768]{2,1,0:T(8,128)(2,1)S(1)}, bf16[1,3072,768]{2,1,0:T(8,128)(2,1)}, u32[]{:S(2)}) copy-start(bf16[1,3072,768]{2,1,0:T(8,128)(2,1)} %param.38) | copy-start | bytes 14155780
  203.2 27.6 %all-to-all-start.1 = ((bf16[8,144,768]{2,1,0:T(8,128)(2,1)}), bf16[8,144,768]{2,1,0:T(8,128)(2,1)}, u32[]{:S(2)}, u32[]{:S(2)}) async-start(bf16[8,144,768]{2,1,0:T(8,128)(2,1)} %bitcast.176), calls=%async_computation.1 | async-start | bytes 3538944 | tf_op jit(solution)/shard_map/all_to_all | solution.py:197
  207.7 135.9 %reduce-scatter.15.cloned.1.call-start = ((), (), s32[]{:S(2)}) async-start(), calls=%async_computation.11 | async-start | bytes 245760
  278.8 67.6 %reduce-scatter.13.cloned.1.call-start = ((), (), s32[]{:S(2)}) async-start(), calls=%async_computation.10 | async-start | bytes 983040
  301.7 291.7 %reduce-scatter.11.cloned.1.call-start = ((), (), s32[]{:S(2)}) async-start(), calls=%async_computation.9 | async-start | bytes 5898240 | tf_op jit(solution)/shard_map/reduce_scatter | solution.py:247
  324.2 27.6 %all-to-all-start.3 = ((bf16[8,144,768]{2,1,0:T(8,128)(2,1)}), bf16[8,144,768]{2,1,0:T(8,128)(2,1)}, u32[]{:S(2)}, u32[]{:S(2)}) async-start(bf16[8,144,768]{2,1,0:T(8,128)(2,1)} %bitcast.174), calls=%async_computation.3 | async-start | bytes 3538944 | tf_op jit(solution)/shard_map/all_to_all | solution.py:233
  328.7 267.6 %reduce-scatter.9.cloned.1.call-start = ((), (), s32[]{:S(2)}) async-start(), calls=%async_computation.8 | async-start | bytes 5898240 | tf_op jit(solution)/shard_map/reduce_scatter | solution.py:241
  343.5 362.0 %all-reduce.4.cloned.1.call-start = ((), (), s32[]{:S(2)}) async-start(), calls=%async_computation.12 | async-start | bytes 18874368 | tf_op jit(solution)/shard_map/psum | solution.py:302
  351.8 10.1 %slice-start = ((s8[7077888]{0:T(1024)(128)(4,1)}), s8[4194304]{0:T(1024)(128)(4,1)S(1)}, s32[]{:S(2)}) async-start(s8[7077888]{0:T(1024)(128)(4,1)} %bitcast.164), calls=%async_computation.13 | async-start | bytes 8388608
  351.9 10.0 %slice-start.1 = ((s8[7077888]{0:T(1024)(128)(4,1)}), s8[2883584]{0:T(1024)(128)(4,1)S(1)}, s32[]{:S(2)}) async-start(s8[7077888]{0:T(1024)(128)(4,1)} %bitcast.164), calls=%async_computation.14 | async-start | bytes 5767168
  372.1 131.4 %copy-start.32 = (f32[1152]{0:T(1024)S(1)}, f32[1152]{0:T(1024)}, u32[]{:S(2)}) copy-start(f32[1152]{0:T(1024)} %copy-done.31) | copy-start | bytes 13828
  372.1 131.4 %copy-start.39 = (f32[1152]{0:T(1024)S(1)}, f32[1152]{0:T(1024)}, u32[]{:S(2)}) copy-start(f32[1152]{0:T(1024)} %copy-done.38) | copy-start | bytes 13828
  (53 other events, 218.7 us)
Sparse Core Ops, SparseCore 0:
  278.9 19.2 reduce-scatter.14
  301.9 23.1 reduce-scatter.12
  327.4 84.5 reduce-scatter.10
  414.1 85.8 reduce-scatter.8
Sparse Core Ops, SparseCore 1:
  514.7 190.8 all-reduce.3
where the time goes:
time: 728 us; the launch traced here: 721 us
  matrix products  275 us (38%)
  waiting for transfers between devices  141 us (19%)
  local copies, waits for them, and re-layouts  108 us (15%)
  other arithmetic  96.2 us (13%)
  blocking collectives  67.9 us (9%)
  between operations  16.1 us (2%)
  starting transfers between devices  14.7 us (2%)
    psum x1, waiting for transfers between devices, on_device(): lax.psum((local_qkv, local_q_bias, local_v_bias, local_proj, local_proj_b...  106 us
    unnamed x123, local copies, waits for them, and re-layouts  48.4 us
    dot_general x6, matrix products, contract_first(): lax.dot_general(left, right, (((0,), (0,)), ((), ())), preferred_element_...  44.9 us
    dot_general x4, matrix products, contract_last(): lax.dot_general(left, right, (((1,), (1,)), ((), ())), preferred_element_...  43.2 us
    psum x1, blocking collectives, on_device(): lax.psum((local_qkv, local_q_bias, local_v_bias, local_proj, local_proj_b...  41.6 us
    dot_general x1, matrix products, on_device(): jnp.dot(arrived, weight_in, preferred_element_type=jnp.float32) + bias_in  40.7 us
    dot_general x4, matrix products, image_scores(): jnp.einsum('qhd,khd->hqk', by_heads(queries), by_heads(key_rows), preferr...  31.1 us
    all_to_all x1, blocking collectives, on_device(): lax.all_to_all(grad_returned, 'exp', split_axis=0, concat_axis=0, tiled=T...  26.2 us
  transfers between devices with their start and end apart: 8, of which 4 were waited for; matrix products, arithmetic and copies ran while one was open for 39% of the time, Pallas kernels for 0%

commit v1 on v0

--- a/solution.py
+++ b/solution.py
@@ -300,19 +300,22 @@
         grad_shift_two,
         grad_w_router,
     ) = lax.psum(
-        (
-            local_qkv,
-            local_q_bias,
-            local_v_bias,
-            local_proj,
-            local_proj_bias,
-            local_gain_one,
-            local_shift_one,
-            local_gain_two,
-            local_shift_two,
-            local_router,
+        lax.psum(
+            (
+                local_qkv,
+                local_q_bias,
+                local_v_bias,
+                local_proj,
+                local_proj_bias,
+                local_gain_one,
+                local_shift_one,
+                local_gain_two,
+                local_shift_two,
+                local_router,
+            ),
+            "exp",
         ),
-        ("rep", "exp"),
+        "rep",
     )
     return (
         mixed,

time: 728 us -> 1070 us (1.47)
  waiting for transfers between devices: 141 us -> 481 us
    psum x0 -> x1, waiting for transfers between devices: none -> 315 us  [on_device(): lax.psum(lax.psum((local_qkv, local_q_bias, local_v_bias, local_proj, loc...]
    psum x0 -> x1, blocking collectives: none -> 21.9 us  [on_device(): lax.psum(lax.psum((local_qkv, local_q_bias, local_v_bias, local_proj, loc...]
    all_to_all x1, waiting for transfers between devices: 2.62 us -> 21.8 us  [on_device(): lax.all_to_all(grad_arrived, 'exp', split_axis=0, concat_axis=0, tiled=True)]
    psum x1, blocking collectives: 41.6 us -> 26.2 us  [on_device(): lax.psum((local_qkv, local_q_bias, local_v_bias, local_proj, local_proj_b...]
    unnamed x123 -> x131, local copies, waits for them, and re-layouts: 48.4 us -> 47.4 us
  transfers between devices with their start and end apart: 8 -> 9, of which waited for: 4 -> 5; matrix products, arithmetic and copies ran while one was open for 39% -> 8% of each run, Pallas kernels for 0% -> 0%
where the time goes in v1:
time: 1070 us; the launch traced here: 1060 us
  waiting for transfers between devices  481 us (45%)
  matrix products  274 us (26%)
  local copies, waits for them, and re-layouts  107 us (10%)
  other arithmetic  92.3 us (9%)
  blocking collectives  74.6 us (7%)
  between operations  16.9 us (2%)
  starting transfers between devices  15.4 us (1%)
    psum x1, waiting for transfers between devices, on_device(): lax.psum(lax.psum((local_qkv, local_q_bias, local_v_bias, local_proj, loc...  315 us
    psum x1, waiting for transfers between devices, on_device(): lax.psum((local_qkv, local_q_bias, local_v_bias, local_proj, local_proj_b...  112 us
    unnamed x131, local copies, waits for them, and re-layouts  47.4 us
    dot_general x6, matrix products, contract_first(): lax.dot_general(left, right, (((0,), (0,)), ((), ())), preferred_element_...  44.8 us
    dot_general x4, matrix products, contract_last(): lax.dot_general(left, right, (((1,), (1,)), ((), ())), preferred_element_...  42.6 us
    dot_general x1, matrix products, on_device(): jnp.dot(arrived, weight_in, preferred_element_type=jnp.float32) + bias_in  40.7 us
    dot_general x4, matrix products, image_scores(): jnp.einsum('qhd,khd->hqk', by_heads(queries), by_heads(key_rows), preferr...  31 us
    all_to_all x1, blocking collectives, on_device(): lax.all_to_all(grad_returned, 'exp', split_axis=0, concat_axis=0, tiled=T...  26.5 us
  transfers between devices with their start and end apart: 9, of which 5 were waited for; matrix products, arithmetic and copies ran while one was open for 8% of the time, Pallas kernels for 0%

profile of v1, /device:TPU:0, one launch (start us, length us, event | category | flops | bytes accessed | tf_op | source)
XLA Modules:
  0.0 1062.2 jit_solution(18850700597638353)
XLA Ops:
  40.2 75.8 %while.22 = (s32[]{:T(128)}, bf16[2,576,768]{2,1,0:T(8,128)(2,1)}, f32[2,12,576]{2,1,0:T(8,128)}, bf16[2,576,768]{1,2,0:T(8,128)(2,1)}, bf16[2,576,768]{1,2,0:T(...) while((s32[]{:T(128)}, bf16[2,576,768]{2,1,0:T(8,128)(2,1)}, f32[2,12,576]{2,1,0:T(8,128)}, ...), condition=%wide.region_5.6_spmd, body=%wide.region_2.5_spmd.sunk | while | flops 1055040768 | bytes 61086932 | solution.py:159
  62.0 11.1 %fusion.144 = bf16[12,64,576]{2,1,0:T(8,128)(2,1)} fusion(bf16[576,12,64]{0,2,1:T(8,128)(2,1)} %bitcast.167, f32[12,576,576]{1,2,0:T(8,128)} %get-tuple-element.357, f32[12,576]{1,0:T(8,128)} %fusion.143, f32[12,576]{1,0:T(8,128)} %get-tuple-element.358), kind=kOutput, calls=%fused_computation.4.clone.1 | convolution fusion | flops 525533184 | bytes 17750016 | tf_op jit(solution)/shard_map/while/body/eval_jaxpr/hqk,khd->qhd/dot_general | solution.py:72
  99.7 11.1 %fusion.144 = bf16[12,64,576]{2,1,0:T(8,128)(2,1)} fusion(bf16[576,12,64]{0,2,1:T(8,128)(2,1)} %bitcast.167, f32[12,576,576]{1,2,0:T(8,128)} %get-tuple-element.357, f32[12,576]{1,0:T(8,128)} %fusion.143, f32[12,576]{1,0:T(8,128)} %get-tuple-element.358), kind=kOutput, calls=%fused_computation.4.clone.1 | convolution fusion | flops 525533184 | bytes 17750016 | tf_op jit(solution)/shard_map/while/body/eval_jaxpr/hqk,khd->qhd/dot_general | solution.py:72
  141.1 14.5 %all-to-all-done = bf16[8,144,768]{2,1,0:T(8,128)(2,1)} async-done(((bf16[8,144,768]{2,1,0:T(8,128)(2,1)}), bf16[8,144,768]{2,1,0:T(8,128)(2,1)}, u32[]{:S(2)}, u32[]{:S(2)}) %all-to-all-start) | async-done | bytes 1769504 | tf_op jit(solution)/shard_map/all_to_all | solution.py:185
  155.7 40.7 %multiply_convert_fusion.3 = (bf16[1152,3072]{1,0:T(8,128)(2,1)S(1)}, f32[1152,3072]{1,0:T(8,128)}, f32[1152,3072]{1,0:T(8,128)}) fusion(f32[3072]{0:T(1024)S(1)} %bitcast.180, bf16[1152,768]{1,0:T(8,128)(2,1)} %bitcast.20, bf16[1,768,3072]{2,1,0:T(8,128)(2,1)} %param.36), kind=kOutput, calls=%fused_computation.32 | convolution fusion | flops 5669388288 | bytes 41889792 | tf_op jit(solution)/shard_map/dot_general | solution.py:192
  213.0 18.0 %all-to-all-done.1 = bf16[8,144,768]{2,1,0:T(8,128)(2,1)} async-done(((bf16[8,144,768]{2,1,0:T(8,128)(2,1)}), bf16[8,144,768]{2,1,0:T(8,128)(2,1)}, u32[]{:S(2)}, u32[]{:S(2)}) %all-to-all-start.1) | async-done | bytes 1769504 | tf_op jit(solution)/shard_map/all_to_all | solution.py:197
  248.7 26.5 %all_to_all.20 = bf16[8,144,768]{2,1,0:T(8,128)(2,1)} all-to-all(bf16[8,144,768]{2,1,0:T(8,128)(2,1)S(1)} %bitcast.177), channel_id=1, replica_groups=mesh['rep'=4,'exp'=8] {'exp'}, dimensions={0} | all-to-all | bytes 3538944 | tf_op jit(solution)/shard_map/all_to_all | solution.py:224
  275.2 20.3 %fusion.86 = (bf16[3072]{0:T(1024)(128)(2,1)}, bf16[1152,3072]{1,0:T(8,128)(2,1)}) fusion(f32[1152,3072]{1,0:T(8,128)} %get-tuple-element.247, f32[1152,3072]{1,0:T(8,128)} %get-tuple-element.264, bf16[1152,768]{1,0:T(8,128)(2,1)} %bitcast.169, bf16[1,3072,768]{2,1,0:T(8,128)(2,1)} %param.38), kind=kOutput, calls=%fused_computation.154 | convolution fusion | flops 5488899072 | bytes 41883648 | tf_op jit(solution)/shard_map/dot_general | solution.py:38
  295.5 10.3 fusion.55
  311.4 21.8 %all-to-all-done.3 = bf16[8,144,768]{2,1,0:T(8,128)(2,1)} async-done(((bf16[8,144,768]{2,1,0:T(8,128)(2,1)}), bf16[8,144,768]{2,1,0:T(8,128)(2,1)}, u32[]{:S(2)}, u32[]{:S(2)}) %all-to-all-start.3) | async-done | bytes 1769504 | tf_op jit(solution)/shard_map/all_to_all | solution.py:233
  353.5 129.7 %while.23 = (s32[]{:T(128)}, bf16[2,576,2304]{2,1,0:T(8,128)(2,1)}, bf16[2,576,768]{1,2,0:T(8,128)(2,1)}, bf16[2,576,768]{1,2,0:T(8,128)(2,1)}, f32[2,12,576]{2,...) while((s32[]{:T(128)}, bf16[2,576,2304]{2,1,0:T(8,128)(2,1)}, ...), condition=%wide.region_19.20_spmd, body=%wide.region_17.19_spmd.sunk | while | flops 2605982976 | bytes 160441552 | solution.py:271
  369.9 10.1 fusion.156
  380.0 11.6 %multiply_reduce_fusion.11 = (f32[12,576]{1,0:T(8,128)S(1)}, f32[12,576,576]{1,2,0:T(8,128)}) fusion(f32[12,576,576]{1,2,0:T(8,128)} %fusion.155, f32[12,576]{1,0:T(8,128)S(1)} %copy-done.11, bf16[576,12,64]{0,2,1:T(8,128)(2,1)S(1)} %bitcast.155, bf16[576,12,64]{0,2,1:T(8,128)(2,1)S(1)} %bitcast.160), kind=kOutput, calls=%fused_computation.12.clone.1 | convolution fusion | flops 525526272 | bytes 33675264 | tf_op jit(solution)/shard_map/while/body/eval_jaxpr/qhd,khd->hqk/dot_general | solution.py:84
  391.7 12.4 %multiply_convert_fusion.7 = bf16[12,576,576]{1,2,0:T(8,128)(2,1)S(1)} fusion(f32[12,576,576]{1,2,0:T(8,128)} %get-tuple-element.368, f32[12,576,576]{1,2,0:T(8,128)} %fusion.155, f32[12,576]{1,0:T(8,128)S(1)} %get-tuple-element.369, f32[12,576]{1,0:T(8,128)S(1)} %copy-done.11), kind=kLoop, calls=%fused_computation.11.clone.1 | loop fusion | flops 19906560 | bytes 39868416 | tf_op jit(solution)/shard_map/while/body/eval_jaxpr/convert_element_type | solution.py:92
  434.5 10.1 fusion.156
  444.7 11.6 %multiply_reduce_fusion.11 = (f32[12,576]{1,0:T(8,128)S(1)}, f32[12,576,576]{1,2,0:T(8,128)}) fusion(f32[12,576,576]{1,2,0:T(8,128)} %fusion.155, f32[12,576]{1,0:T(8,128)S(1)} %copy-done.11, bf16[576,12,64]{0,2,1:T(8,128)(2,1)S(1)} %bitcast.155, bf16[576,12,64]{0,2,1:T(8,128)(2,1)S(1)} %bitcast.160), kind=kOutput, calls=%fused_computation.12.clone.1 | convolution fusion | flops 525526272 | bytes 33675264 | tf_op jit(solution)/shard_map/while/body/eval_jaxpr/qhd,khd->hqk/dot_general | solution.py:84
  456.3 12.4 %multiply_convert_fusion.7 = bf16[12,576,576]{1,2,0:T(8,128)(2,1)S(1)} fusion(f32[12,576,576]{1,2,0:T(8,128)} %get-tuple-element.368, f32[12,576,576]{1,2,0:T(8,128)} %fusion.155, f32[12,576]{1,0:T(8,128)S(1)} %get-tuple-element.369, f32[12,576]{1,0:T(8,128)S(1)} %copy-done.11), kind=kLoop, calls=%fused_computation.11.clone.1 | loop fusion | flops 19906560 | bytes 39868416 | tf_op jit(solution)/shard_map/while/body/eval_jaxpr/convert_element_type | solution.py:92
  483.2 11.1 %fusion.78 = f32[768,2304]{1,0:T(8,128)} fusion(bf16[1152,2304]{1,0:T(8,128)(2,1)} %bitcast.172, bf16[1152,768]{0,1:T(8,128)(2,1)} %copy.98, f32[768]{0:T(1024)} %param.32, f32[768]{0:T(1024)} %param.31, f32[1152]{0:T(1024)S(1)} %copy-done.42, f32[1152]{0:T(1024)S(1)} %copy-done.32), kind=kOutput, calls=%fused_computation.149 | convolution fusion | flops 4082171904 | bytes 14171136 | tf_op jit(solution)/shard_map/dot_general | solution.py:44
  499.2 11.1 %fusion.28 = bf16[1,3072,768]{2,1,0:T(8,128)(2,1)} fusion(bf16[1152,3072]{1,0:T(8,128)(2,1)} %copy-done.63, bf16[1152,768]{1,0:T(8,128)(2,1)} %bitcast.170), kind=kOutput, calls=%fused_computation.71 | convolution fusion | flops 5438177280 | bytes 13565952 | tf_op jit(solution)/shard_map/dot_general | solution.py:44
  510.4 10.7 %fusion.27 = bf16[1,768,3072]{2,1,0:T(8,128)(2,1)} fusion(bf16[1152,768]{1,0:T(8,128)(2,1)} %bitcast.20, bf16[1152,3072]{1,0:T(8,128)(2,1)} %get-tuple-element.271), kind=kOutput, calls=%fused_computation.70 | convolution fusion | flops 5438177280 | bytes 13565952 | tf_op jit(solution)/shard_map/dot_general | solution.py:44
  521.1 111.5 %all-reduce.7.cloned.1.call-done = (f32[768,2304]{1,0:T(8,128)}, f32[768,768]{1,0:T(8,128)}) async-done(((f32[768,2304]{1,0:T(8,128)}, f32[768,768]{1,0:T(8,128)}), (f32[768,2304]{1,0:T(8,128)}, f32[768,768]{1,0:T(8,128)})) %all-reduce.7.cloned.1.call-update) | async-done | bytes 9437200 | tf_op jit(solution)/shard_map/psum | solution.py:303
  677.2 26.2 %all-reduce = (f32[768]{0:T(1024)}, f32[768]{0:T(1024)}, f32[768]{0:T(1024)}, f32[768]{0:T(1024)}, f32[768]{0:T(1024)}, /*index=5*/f32[768]{0:T(1024)}, f32[768]{0:T(1024)}, f32[768,8]{0,1:T(8,128)}) all-reduce(f32[768]{0:T(1024)S(1)} %get-tuple-element.182, ...), channel_id=1, replica_groups=mesh['rep'=4,'exp'=8] {'exp'}, use_global_device_ids=true, to_apply=%region_25.26 | all-reduce | flops 11520 | bytes 92160 | tf_op jit(solution)/shard_map/psum | solution.py:303
  703.5 21.9 %all-reduce.2 = (f32[768]{0:T(1024)}, f32[768]{0:T(1024)}, f32[768]{0:T(1024)}, f32[768]{0:T(1024)}, f32[768]{0:T(1024)}, /*index=5*/f32[768]{0:T(1024)}, f32[768]{0:T(1024)}, f32[768,8]{0,1:T(8,128)}) all-reduce(f32[768]{0:T(1024)} %get-tuple-element.224, f32[768]{0:T(1024)} %get-tuple-element.225, ...), channel_id=1, replica_groups=mesh['rep'=4,'exp'=8] {'rep'}, use_global_device_ids=true, to_apply=%region_26.27 | all-reduce | flops 11520 | bytes 92160 | tf_op jit(solution)/shard_map/psum | solution.py:302
  731.3 314.8 %all-reduce.9.cloned.1.call-done = (f32[768,2304]{1,0:T(8,128)}, f32[768,768]{1,0:T(8,128)}) async-done(((f32[768,2304]{1,0:T(8,128)}, f32[768,768]{1,0:T(8,128)}), (f32[768,2304]{1,0:T(8,128)}, f32[768,768]{1,0:T(8,128)})) %all-reduce.9.cloned.1.call-update) | async-done | bytes 9437200 | tf_op jit(solution)/shard_map/psum | solution.py:302
  (275 shorter events, 294.5 us)
Async XLA Ops:
  8.0 12.2 %copy-start = (bf16[768,2304]{1,0:T(8,128)(2,1)S(1)}, bf16[768,2304]{1,0:T(8,128)(2,1)}, u32[]{:S(2)}) copy-start(bf16[768,2304]{1,0:T(8,128)(2,1)} %param.26) | copy-start | bytes 10616836
  40.2 75.8 %copy-start.56 = (f32[768]{0:T(1024)S(1)}, f32[768]{0:T(1024)}, u32[]{:S(2)}) copy-start(f32[768]{0:T(1024)} %convert_element_type.153) | copy-start | bytes 9220
  62.0 11.1 %copy-start.14 = (f32[12,576]{1,0:T(8,128)S(1)}, f32[12,576]{1,0:T(8,128)}, u32[]{:S(2)}) copy-start(f32[12,576]{1,0:T(8,128)} %get-tuple-element.358) | copy-start | bytes 82948 | tf_op jit(solution)/shard_map/while
  62.0 11.1 %copy-start.15 = (f32[12,576]{1,0:T(8,128)S(1)}, f32[12,576]{1,0:T(8,128)}, u32[]{:S(2)}) copy-start(f32[12,576]{1,0:T(8,128)} %fusion.143) | copy-start | bytes 82948 | tf_op jit(solution)/shard_map/while
  62.0 11.1 %copy-start.23 = (f32[2,12,576]{2,1,0:T(8,128)S(1)}, f32[2,12,576]{2,1,0:T(8,128)}, u32[]{:S(2)}) copy-start(f32[2,12,576]{2,1,0:T(8,128)} %get-tuple-element.379) | copy-start | bytes 165892 | tf_op jit(solution)/shard_map/while
  99.7 11.1 %copy-start.14 = (f32[12,576]{1,0:T(8,128)S(1)}, f32[12,576]{1,0:T(8,128)}, u32[]{:S(2)}) copy-start(f32[12,576]{1,0:T(8,128)} %get-tuple-element.358) | copy-start | bytes 82948 | tf_op jit(solution)/shard_map/while
  99.7 11.1 %copy-start.15 = (f32[12,576]{1,0:T(8,128)S(1)}, f32[12,576]{1,0:T(8,128)}, u32[]{:S(2)}) copy-start(f32[12,576]{1,0:T(8,128)} %fusion.143) | copy-start | bytes 82948 | tf_op jit(solution)/shard_map/while
  99.7 11.1 %copy-start.23 = (f32[2,12,576]{2,1,0:T(8,128)S(1)}, f32[2,12,576]{2,1,0:T(8,128)}, u32[]{:S(2)}) copy-start(f32[2,12,576]{2,1,0:T(8,128)} %get-tuple-element.379) | copy-start | bytes 165892 | tf_op jit(solution)/shard_map/while
  126.6 10.4 copy-start.58
  126.6 29.0 %all-to-all-start = ((bf16[8,144,768]{2,1,0:T(8,128)(2,1)}), bf16[8,144,768]{2,1,0:T(8,128)(2,1)}, u32[]{:S(2)}, u32[]{:S(2)}) async-start(bf16[8,144,768]{2,1,0:T(8,128)(2,1)} %bitcast.174), calls=%async_computation | async-start | bytes 3538944 | tf_op jit(solution)/shard_map/all_to_all | solution.py:185
  133.1 22.6 %copy-start.54 = (f32[1,3072]{1,0:T(1,128)S(1)}, f32[1,3072]{1,0:T(1,128)}, u32[]{:S(2)}) copy-start(f32[1,3072]{1,0:T(1,128)} %add.197) | copy-start | bytes 36868
  155.7 40.7 %copy-start.55 = (f32[768]{0:T(1024)S(1)}, f32[768]{0:T(1024)}, u32[]{:S(2)}) copy-start(f32[768]{0:T(1024)} %convert_reduce_fusion.2) | copy-start | bytes 9220
  155.7 40.7 %copy-start.59 = (bf16[1,3072,768]{2,1,0:T(8,128)(2,1)S(1)}, bf16[1,3072,768]{2,1,0:T(8,128)(2,1)}, u32[]{:S(2)}) copy-start(bf16[1,3072,768]{2,1,0:T(8,128)(2,1)} %param.38) | copy-start | bytes 14155780
  203.2 27.8 %all-to-all-start.1 = ((bf16[8,144,768]{2,1,0:T(8,128)(2,1)}), bf16[8,144,768]{2,1,0:T(8,128)(2,1)}, u32[]{:S(2)}, u32[]{:S(2)}) async-start(bf16[8,144,768]{2,1,0:T(8,128)(2,1)} %bitcast.176), calls=%async_computation.1 | async-start | bytes 3538944 | tf_op jit(solution)/shard_map/all_to_all | solution.py:197
  305.8 27.5 %all-to-all-start.3 = ((bf16[8,144,768]{2,1,0:T(8,128)(2,1)}), bf16[8,144,768]{2,1,0:T(8,128)(2,1)}, u32[]{:S(2)}, u32[]{:S(2)}) async-start(bf16[8,144,768]{2,1,0:T(8,128)(2,1)} %bitcast.175), calls=%async_computation.3 | async-start | bytes 3538944 | tf_op jit(solution)/shard_map/all_to_all | solution.py:233
  310.1 322.5 %all-reduce.7.cloned.1.call-start = ((), (), s32[]{:S(2)}) async-start(), calls=%async_computation.12 | async-start | bytes 18874368 | tf_op jit(solution)/shard_map/psum | solution.py:303
  311.4 26.8 %copy-start.34 = (f32[1152]{0:T(1024)}, f32[1152]{0:T(1024)S(1)}, u32[]{:S(2)}) copy-start(f32[1152]{0:T(1024)S(1)} %multiply_reduce_fusion.7) | copy-start | bytes 13828
  353.5 129.7 %copy-start.32 = (f32[1152]{0:T(1024)S(1)}, f32[1152]{0:T(1024)}, u32[]{:S(2)}) copy-start(f32[1152]{0:T(1024)} %copy-done.31) | copy-start | bytes 13828
  353.5 129.7 %copy-start.42 = (f32[1152]{0:T(1024)S(1)}, f32[1152]{0:T(1024)}, u32[]{:S(2)}) copy-start(f32[1152]{0:T(1024)} %copy-done.41) | copy-start | bytes 13828
  494.3 142.6 %reduce-scatter.15.cloned.1.call-start = ((), (), s32[]{:S(2)}) async-start(), calls=%async_computation.11 | async-start | bytes 245760
  497.1 141.4 %reduce-scatter.13.cloned.1.call-start = ((), (), s32[]{:S(2)}) async-start(), calls=%async_computation.10 | async-start | bytes 983040
  499.2 226.2 %reduce-scatter.11.cloned.1.call-start = ((), (), s32[]{:S(2)}) async-start(), calls=%async_computation.9 | async-start | bytes 5898240 | tf_op jit(solution)/shard_map/reduce_scatter | solution.py:247
  510.3 218.1 %reduce-scatter.9.cloned.1.call-start = ((), (), s32[]{:S(2)}) async-start(), calls=%async_computation.8 | async-start | bytes 5898240 | tf_op jit(solution)/shard_map/reduce_scatter | solution.py:241
  521.1 525.1 %all-reduce.9.cloned.1.call-start = ((), (), s32[]{:S(2)}) async-start(), calls=%async_computation.13 | async-start | bytes 18874368 | tf_op jit(solution)/shard_map/psum | solution.py:302
  (58 other events, 252.1 us)
Sparse Core Ops, SparseCore 0:
  494.5 138.1 all-reduce.6
Sparse Core Ops, SparseCore 1:
  497.6 19.3 reduce-scatter.14
  519.8 21.2 reduce-scatter.12
  543.3 84.6 reduce-scatter.10
  630.4 86.9 reduce-scatter.8
  719.9 326.2 all-reduce.8
